TPU v7x, 32 devices: a whole 2x2x4 slice. The times are simulated.
32 devices in a mesh: lat: 4 (over y, x), lon: 8 (over z, core).
Axes of the slice: x: 2, y: 2, z: 4, core: 2. Of those that a mesh axis runs over, the one named last changes fastest.
Arguments:
- fields_in: bfloat16 [8, 1440, 512], P('lat', 'lon'), may hold values from -6 to 6
- span: int32 [8, 5], P('lat'), may hold values from 0 to 7, as said below
- filters: float32 [8, 5, 8, 13], P('lat'), may hold values from -0.9 to 0.9
- basis: float32 [8, 512], replicated, may hold values from -2.1 to 2.1
- w_in: bfloat16 [512, 1024], replicated, may hold values from -0.25 to 0.25
- w_out: bfloat16 [1024, 512], replicated, may hold values from -0.1875 to 0.1875
- cotangent: bfloat16 [8, 1440, 512], P('lat', 'lon'), may hold values from -6 to 6
Outputs:
- result: bfloat16 [8, 1440, 512], P('lat', 'lon')
- grad_fields: bfloat16 [8, 1440, 512], P('lat', 'lon')
- grad_in_w: float32 [512, 1024], replicated
- grad_out_w: float32 [1024, 512], replicated
- grad_basis: float32 [8, 512], replicated
Inputs may be any that keep to these rules, and one draw needn't show every extreme that they name: span[i, d] bounds the used taps: longitude offsets t - 6 with |t - 6| < span[i, d] are in the support; 0 means row i has no support at band offset d.
All inputs are finite; a program needn't handle non-finite values.
Results may differ from a plain program's by a relative error of at most 0.0085.
Values may be sent and summed in bfloat16 or wider, within the bound.
A program may use at most 128 MiB of HBM per device.

v0:
```python
import math

import jax
import jax.numpy as jnp
from jax import lax
from jax.sharding import PartitionSpec as P


def shifted(value, axis, steps):
    count = lax.axis_size(axis)
    leading, last = (max(0, -steps), min(count, count - steps))
    return lax.ppermute(value, axis, [(source, source + steps) for source in range(leading, last)])


def padded(block, sides, width):
    for axis, dim in sides:
        count = lax.axis_size(axis)
        forward = [(i, i + 1) for i in range(count - 1)]
        backward = [(target, source) for source, target in forward]
        low = lax.ppermute(
            lax.slice_in_dim(block, block.shape[dim] - width, None, axis=dim), axis, forward
        )
        high = lax.ppermute(lax.slice_in_dim(block, 0, width, axis=dim), axis, backward)
        block = jnp.concatenate([low, block, high], axis=dim)
    return block


def tap_mask(filters, span):
    reach = (filters.shape[3] - 1) // 2
    offsets = jnp.arange(2 * reach + 1) - reach
    mask = (jnp.abs(offsets)[None, None, :] < span[:, :, None]).astype(jnp.float32)
    return filters * mask[:, :, None, :]


def band_terms(coeff, bands, count, field_view):
    reach = (count - 1) // 2
    outputs = []
    for band_step in range(bands):
        running = coeff(band_step, 0) * field_view(-reach)
        for tap_step in range(1, count):
            running = running + coeff(band_step, tap_step) * field_view(tap_step - reach)
        outputs.append(running.astype(jnp.bfloat16))
    return jnp.stack(outputs, axis=1)


def fold_rows(terms):
    rows = terms.shape[0]
    bands = terms.shape[1]
    extended = jnp.zeros((rows + bands - 1, terms.shape[2], terms.shape[3]), jnp.float32)
    rounded = lax.optimization_barrier(terms).astype(jnp.float32)
    for band_step in range(bands):
        extended = extended.at[band_step : band_step + rows].add(rounded[:, band_step])
    return extended


def settle(extended, band_reach):
    rows = extended.shape[0] - 2 * band_reach
    upper = shifted(extended[rows + band_reach :].astype(jnp.bfloat16), "lat", 1).astype(
        jnp.float32
    )
    lower = shifted(extended[:band_reach].astype(jnp.bfloat16), "lat", -1).astype(jnp.float32)
    inner = extended[band_reach : band_reach + rows]
    inner = inner.at[:band_reach].add(upper)
    return inner.at[rows - band_reach :].add(lower)


def conv_grads(coeff, rows, bands, count, band_view, field_view, lon_axis):
    reach = (count - 1) // 2
    back = None
    tap_grads = []
    for band_step in range(bands):
        centred = band_view(band_step, 0)
        for tap_step in range(count):
            offset = tap_step - reach
            product = coeff(band_step, tap_step) * band_view(band_step, -offset)
            back = product if back is None else back + product
            tap_grads.append(jnp.sum(centred * field_view(offset), axis=lon_axis))
    tap_grad = jnp.stack(tap_grads, axis=1).reshape(rows, bands, count, -1)
    return (back, tap_grad)


def local(fields_in, span, filters, basis, w_in, w_out, cotangent):
    highest = lax.Precision.HIGHEST
    rows, width, channels = fields_in.shape
    masked = tap_mask(filters, span)
    taps = jnp.einsum("rdkt,kc->rdtc", masked, basis, precision=highest)
    reach = (filters.shape[3] - 1) // 2
    count = 2 * reach + 1
    band_reach = (span.shape[1] - 1) // 2
    bands = 2 * band_reach + 1
    lon_count = lax.axis_size("lon")
    slot = lax.axis_index("lon")
    slice_width = channels // lon_count
    lanes_lon = jnp.swapaxes(fields_in, 1, 2)
    cycle = lax.all_to_all(lanes_lon, "lon", split_axis=1, concat_axis=2, tiled=True)
    cycle_taps = lax.dynamic_slice_in_dim(taps, slot * slice_width, slice_width, 3)
    cycle_coeff = lambda band_step, tap_step: cycle_taps[:, band_step, tap_step, :, None]
    cycle_field = lambda offset: jnp.roll(cycle, -offset, axis=2).astype(jnp.float32)
    terms = band_terms(cycle_coeff, bands, count, cycle_field)
    returned = lax.all_to_all(terms, "lon", split_axis=3, concat_axis=2, tiled=True)
    conv = jnp.swapaxes(settle(fold_rows(returned), band_reach), 1, 2)
    hidden_in = (fields_in.astype(jnp.float32) + conv).astype(jnp.bfloat16)
    flat_rows = hidden_in.reshape(-1, channels)
    pre_act = jnp.dot(flat_rows, w_in, preferred_element_type=jnp.float32)
    activated = jax.nn.gelu(pre_act).astype(jnp.bfloat16)
    mixed = jnp.dot(activated, w_out, preferred_element_type=jnp.float32)
    result = (
        (flat_rows.astype(jnp.float32) + mixed).astype(jnp.bfloat16).reshape(rows, width, channels)
    )
    cotangent_flat = cotangent.reshape(-1, channels)
    leading = (((0,), (0,)), ((), ()))
    trailing = (((1,), (1,)), ((), ()))
    grad_out_w = lax.dot_general(
        activated, cotangent_flat, leading, preferred_element_type=jnp.float32
    )
    grad_act = lax.dot_general(cotangent_flat, w_out, trailing, preferred_element_type=jnp.float32)
    unused, gelu_back = jax.vjp(jax.nn.gelu, pre_act)
    grad_pre = gelu_back(grad_act)[0].astype(jnp.bfloat16)
    grad_in_w = lax.dot_general(flat_rows, grad_pre, leading, preferred_element_type=jnp.float32)
    grad_hidden = (
        (
            cotangent_flat.astype(jnp.float32)
            + lax.dot_general(grad_pre, w_in, trailing, preferred_element_type=jnp.float32)
        )
        .astype(jnp.bfloat16)
        .reshape(rows, width, channels)
    )
    widened = padded(grad_hidden, (("lat", 0),), band_reach)
    grad_cycle = lax.all_to_all(
        jnp.swapaxes(widened, 1, 2), "lon", split_axis=1, concat_axis=2, tiled=True
    )
    cycle_band = lambda band_step, offset: jnp.roll(
        grad_cycle[band_step : band_step + rows], -offset, axis=2
    ).astype(jnp.float32)
    back, tap_grad = conv_grads(cycle_coeff, rows, bands, count, cycle_band, cycle_field, 2)
    back = lax.all_to_all(back.astype(jnp.bfloat16), "lon", split_axis=2, concat_axis=1, tiled=True)
    back = jnp.swapaxes(back, 1, 2)
    slice_basis = jnp.einsum("rdkt,rdtc->kc", masked, tap_grad, precision=highest)
    partial_basis = lax.dynamic_update_slice(
        jnp.zeros((basis.shape[0], channels), jnp.float32), slice_basis, (0, slot * slice_width)
    )
    total_in, total_out, total_basis = lax.psum(
        (grad_in_w, grad_out_w, partial_basis), ("lat", "lon")
    )
    factor = 1.0 / math.sqrt(lax.axis_size("lat") * rows * lon_count * width)
    grad_fields = (grad_hidden.astype(jnp.float32) + back.astype(jnp.float32)).astype(jnp.bfloat16)
    return (result, grad_fields, total_in * factor, total_out * factor, total_basis * factor)


def solution(mesh):
    in_specs = (
        P("lat", "lon", None),
        P("lat", None),
        P("lat", None, None, None),
        P(),
        P(),
        P(),
        P("lat", "lon", None),
    )
    out_specs = (P("lat", "lon", None), P("lat", "lon", None), P(), P(), P())
    return jax.shard_map(local, mesh=mesh, in_specs=in_specs, out_specs=out_specs, check_vma=False)
```

profile of v0, /device:TPU:0, one launch (start us, length us, event | category | flops | bytes accessed | tf_op | source)
XLA Modules:
  0.0 515.9 jit_solution(2721084964690570356)
XLA Ops:
  7.2 3.5 copy.365
  10.7 6.3 %all-to-all-start = ((bf16[2,512,180]{2,0,1:T(2,128)(2,1)}), bf16[2,512,180]{2,0,1:T(2,128)(2,1)S(1)}, u32[]{:S(2)}, u32[]{:S(2)}) async-start(bf16[2,512,180]{2,0,1:T(2,128)(2,1)} %bitcast.3), calls=%async_computation | async-start | bytes 1048576 | tf_op jit(solution)/shard_map/all_to_all | solution.py:95
  18.9 13.4 %all-to-all-done = bf16[2,512,180]{2,0,1:T(2,128)(2,1)S(1)} async-done(((bf16[2,512,180]{2,0,1:T(2,128)(2,1)}), bf16[2,512,180]{2,0,1:T(2,128)(2,1)S(1)}, u32[]{:S(2)}, u32[]{:S(2)}) %all-to-all-start) | async-done | bytes 368672 | tf_op jit(solution)/shard_map/all_to_all | solution.py:95
  50.5 5.1 fusion.152
  56.0 3.8 fusion.153
  60.0 4.5 fusion.154
  64.6 3.8 fusion.155
  68.5 3.8 fusion.156
  72.3 8.7 %copy.371 = bf16[2,5,64,1440]{2,0,1,3:T(2,128)(2,1)} copy(bf16[2,5,64,1440]{3,2,0,1:T(8,128)(2,1)} %fusion.156) | data formatting | bytes 3686400 | tf_op jit(solution)/shard_map/stack | solution.py:43
  81.0 6.7 %reshape.1583 = bf16[8,2,57600]{2,1,0:T(2,128)(2,1)S(1)} reshape(bf16[1440,5,2,64]{3,2,1,0:T(2,128)(2,1)} %bitcast.347) | data formatting | bytes 3686400
  87.6 46.7 %all_to_all.60 = bf16[8,2,57600]{2,1,0:T(2,128)(2,1)} all-to-all(bf16[8,2,57600]{2,1,0:T(2,128)(2,1)S(1)} %reshape.1583), channel_id=1, replica_groups=mesh['lat'=4,'lon'=8] {'lon'}, dimensions={0} | all-to-all | bytes 3686400 | tf_op jit(solution)/shard_map/all_to_all | solution.py:100
  134.4 8.1 %reshape.1584 = bf16[1440,5,2,64]{3,2,1,0:T(2,128)(2,1)} reshape(bf16[8,2,57600]{2,1,0:T(2,128)(2,1)} %all_to_all.60) | data formatting | bytes 3686400
  142.4 10.4 %copy.458 = bf16[2,5,64,8,180]{4,2,3,1,0:T(8,128)(2,1)} copy(bf16[2,5,64,8,180]{2,0,1,4,3:T(2,128)(2,1)} %bitcast.348) | data formatting | bytes 3686400 | tf_op jit(solution)/shard_map/all_to_all | solution.py:100
  152.9 2.2 convert_element_type.999
  160.1 5.4 %collective-permute-start = (bf16[2,512,180]{2,1,0:T(8,128)(2,1)}, bf16[2,512,180]{2,1,0:T(8,128)(2,1)}, u32[]{:S(2)}, u32[]{:S(2)}) collective-permute-start(bf16[2,512,180]{2,1,0:T(8,128)(2,1)} %fusion.75), channel_id=1, source_target_pairs={{0,8},{8,16},{16,24},{1,9},{9,17},{17,25},{2,10},{10,18},{18,26},{... | collective-permute-start | bytes 1105928 | tf_op jit(solution)/shard_map/ppermute | solution.py:12
  168.2 7.6 %collective-permute-done.1 = bf16[2,512,180]{2,1,0:T(8,128)(2,1)} collective-permute-done((bf16[2,512,180]{2,1,0:T(8,128)(2,1)}, bf16[2,512,180]{2,1,0:T(8,128)(2,1)}, u32[]{:S(2)}, u32[]{:S(2)}) %collective-permute-start.1) | collective-permute-done | bytes 368672 | tf_op jit(solution)/shard_map/ppermute | solution.py:12
  178.2 3.7 fusion.6
  184.9 12.9 %collective-permute-start.2 = (bf16[2,180,512]{2,1,0:T(8,128)(2,1)S(1)}, bf16[2,180,512]{2,1,0:T(8,128)(2,1)}, u32[]{:S(2)}, u32[]{:S(2)}) collective-permute-start(bf16[2,180,512]{2,1,0:T(8,128)(2,1)S(1)} %reshape.1564), channel_id=1, source_target_pairs={{0,8},{8,16},{16,24},{1,9},{9,17},{17,25},{2,10},{10,18},{18,26},{... | collective-permute-start | bytes 1105928 | tf_op jit(solution)/shard_map/ppermute | solution.py:20
  197.8 3.2 fusion.237
  201.0 2.2 fusion.161
  207.2 3.1 copy.380
  210.3 4.5 all-to-all-start.2
  241.2 136.0 %all-reduce.4.cloned.1.call-done = (f32[512,1024]{1,0:T(8,128)}, f32[1024,512]{1,0:T(8,128)}) async-done(((f32[512,1024]{1,0:T(8,128)}, f32[1024,512]{1,0:T(8,128)}), (f32[512,1024]{1,0:T(8,128)}, f32[1024,512]{1,0:T(8,128)})) %all-reduce.4.cloned.1.call-update) | async-done | bytes 4194320 | tf_op jit(solution)/shard_map/psum | solution.py:142
  377.2 3.4 broadcast_multiply_fusion.1
  394.9 2.1 copy.385
  405.8 2.1 copy.383
  420.2 5.4 %fusion.68 = (f32[2,64]{1,0:T(2,128)}, f32[2,64]{1,0:T(2,128)}, f32[2,64]{1,0:T(2,128)}, f32[2,64]{1,0:T(2,128)}, f32[2,64]{1,0:T(2,128)}, /*index=5*/f32[2,64]{...) fusion(f32[2,64,8,180]{3,2,1,0:T(8,128)S(1)} %copy-done.14, ...), kind=kLoop, calls=%fused_computation.200 | loop fusion | flops 12161280 | bytes 5913600 | tf_op jit(solution)/shard_map/reduce_sum | solution.py:77
  426.4 20.4 %add_convert_fusion = bf16[2,64,1440]{2,1,0:T(8,128)(2,1)} fusion(bf16[2,64,1440]{2,1,0:T(8,128)(2,1)S(1)} %slice.1410, bf16[2,64,1440]{2,1,0:T(8,128)(2,1)S(1)} %slice.1384, bf16[2,64,1440]{2,1,0:T(8,128)(2,1)S(1)} %slice.1358, bf16[2,64,1440]{2,1,0:T(8,128)(2,1)S(1)} %slice.1332, bf16[2,64,1440]{2,1,0:T(8,128)(2,1)S(1)} %slice.1306, ...), kind=kLoop, calls=%fused_computation.287 | loop fusion | flops 69120000 | bytes 24363520 | tf_op jit(solution)/shard_map/convert_element_type | solution.py:136
  446.8 2.6 copy.387
  450.6 3.4 all-to-all-start.3
  454.4 7.0 %fusion.71 = (f32[2,64]{1,0:T(2,128)S(1)}, f32[2,64]{1,0:T(2,128)S(1)}, f32[2,64]{1,0:T(2,128)S(1)}, f32[2,64]{1,0:T(2,128)S(1)}, f32[2,64]{1,0:T(2,128)S(1)}, /...) fusion(f32[2,64,8,180]{3,2,1,0:T(8,128)} %reshape.1576, ...), kind=kLoop, calls=%fused_computation.203 | loop fusion | flops 11976960 | bytes 6282240 | tf_op jit(solution)/shard_map/reduce_sum | solution.py:77
  463.0 40.9 %psum.23 = f32[8,512]{1,0:T(8,128)S(1)} all-reduce(f32[8,512]{1,0:T(8,128)S(1)} %dynamic_update_slice.3), channel_id=1, replica_groups=mesh['lat'=4,'lon'=8] {'lat','lon'}, use_global_device_ids=true, to_apply=%region_67.68 | all-reduce | flops 4096 | bytes 32768 | tf_op jit(solution)/shard_map/psum | solution.py:142
  (563 shorter events, 105.9 us)
Async XLA Ops:
  7.2 171.0 %copy-start = (bf16[512,1024]{1,0:T(8,128)(2,1)S(1)}, bf16[512,1024]{1,0:T(8,128)(2,1)}, u32[]{:S(2)}) copy-start(bf16[512,1024]{1,0:T(8,128)(2,1)} %param.29) | copy-start | bytes 3145732
  7.2 9.9 %copy-start.183 = (s32[2,5]{1,0:T(2,128)S(1)}, s32[2,5]{1,0:T(2,128)}, u32[]{:S(2)}) copy-start(s32[2,5]{1,0:T(2,128)} %param.26) | copy-start | bytes 124
  7.2 10.0 %copy-start.53 = (f32[2,5,8,13]{3,2,1,0:T(8,128)S(1)}, f32[2,5,8,13]{3,2,1,0:T(8,128)}, u32[]{:S(2)}) copy-start(f32[2,5,8,13]{3,2,1,0:T(8,128)} %param.27) | copy-start | bytes 12484
  7.2 9.9 %copy-start.101 = (f32[8,512]{1,0:T(8,128)S(1)}, f32[8,512]{1,0:T(8,128)}, u32[]{:S(2)}) copy-start(f32[8,512]{1,0:T(8,128)} %param.28) | copy-start | bytes 49156
  10.7 21.7 %all-to-all-start = ((bf16[2,512,180]{2,0,1:T(2,128)(2,1)}), bf16[2,512,180]{2,0,1:T(2,128)(2,1)S(1)}, u32[]{:S(2)}, u32[]{:S(2)}) async-start(bf16[2,512,180]{2,0,1:T(2,128)(2,1)} %bitcast.3), calls=%async_computation | async-start | bytes 1048576 | tf_op jit(solution)/shard_map/all_to_all | solution.py:95
  17.0 360.1 %all-reduce.4.cloned.1.call-start = ((), (), s32[]{:S(2)}) async-start(), calls=%async_computation.4 | async-start | bytes 8388608 | tf_op jit(solution)/shard_map/psum | solution.py:142
  18.9 49.5 %copy-start.102 = (f32[2,1,1,64]{3,2,1,0:T(1,128)}, f32[2,1,1,64]{3,2,1,0:T(1,128)S(1)}, u32[]{:S(2)}) copy-start(f32[2,1,1,64]{3,2,1,0:T(1,128)S(1)} %get-tuple-element.447) | copy-start | bytes 1540
  18.9 49.5 %copy-start.103 = (f32[2,1,1,64]{3,2,1,0:T(1,128)}, f32[2,1,1,64]{3,2,1,0:T(1,128)S(1)}, u32[]{:S(2)}) copy-start(f32[2,1,1,64]{3,2,1,0:T(1,128)S(1)} %get-tuple-element.448) | copy-start | bytes 1540
  156.2 9.3 %copy-start.40 = (bf16[2,180,512]{2,0,1:T(2,128)(2,1)S(1)}, bf16[2,180,512]{2,0,1:T(2,128)(2,1)}, u32[]{:S(2)}) copy-start(bf16[2,180,512]{2,0,1:T(2,128)(2,1)} %param.25) | copy-start | bytes 1105924
  158.0 8.4 %copy-start.52 = (bf16[2,180,512]{2,0,1:T(2,128)(2,1)S(1)}, bf16[2,180,512]{2,0,1:T(2,128)(2,1)}, u32[]{:S(2)}) copy-start(bf16[2,180,512]{2,0,1:T(2,128)(2,1)} %param.31) | copy-start | bytes 1105924
  158.0 8.6 %copy-start.49 = (bf16[1024,512]{1,0:T(8,128)(2,1)S(1)}, bf16[1024,512]{1,0:T(8,128)(2,1)}, u32[]{:S(2)}) copy-start(bf16[1024,512]{1,0:T(8,128)(2,1)} %param.30) | copy-start | bytes 3145732
  158.8 17.0 %collective-permute-start.1 = (bf16[2,512,180]{2,1,0:T(8,128)(2,1)}, bf16[2,512,180]{2,1,0:T(8,128)(2,1)}, u32[]{:S(2)}, u32[]{:S(2)}) collective-permute-start(bf16[2,512,180]{2,1,0:T(8,128)(2,1)} %slice.1718), channel_id=1, source_target_pairs={{8,0},{16,8},{24,16},{9,1},{17,9},{25,17},{10,2},{18,10},{26,18},{... | collective-permute-start | bytes 1105928 | tf_op jit(solution)/shard_map/ppermute | solution.py:12
  160.1 16.0 %collective-permute-start = (bf16[2,512,180]{2,1,0:T(8,128)(2,1)}, bf16[2,512,180]{2,1,0:T(8,128)(2,1)}, u32[]{:S(2)}, u32[]{:S(2)}) collective-permute-start(bf16[2,512,180]{2,1,0:T(8,128)(2,1)} %fusion.75), channel_id=1, source_target_pairs={{0,8},{8,16},{16,24},{1,9},{9,17},{17,25},{2,10},{10,18},{18,26},{... | collective-permute-start | bytes 1105928 | tf_op jit(solution)/shard_map/ppermute | solution.py:12
  183.4 22.5 %copy-start.21 = (bf16[2,180,512]{2,1,0:T(8,128)(2,1)}, bf16[2,180,512]{2,1,0:T(8,128)(2,1)S(1)}, u32[]{:S(2)}) copy-start(bf16[2,180,512]{2,1,0:T(8,128)(2,1)S(1)} %reshape.1564) | copy-start | bytes 1105924
  183.4 17.5 %copy-start.184 = (f32[360,1024]{1,0:T(8,128)S(1)}, f32[360,1024]{1,0:T(8,128)}, u32[]{:S(2)}) copy-start(f32[360,1024]{1,0:T(8,128)} %get-tuple-element.513) | copy-start | bytes 4423684
  183.5 22.5 %collective-permute-start.3 = (bf16[2,180,512]{2,1,0:T(8,128)(2,1)S(1)}, bf16[2,180,512]{2,1,0:T(8,128)(2,1)}, u32[]{:S(2)}, u32[]{:S(2)}) collective-permute-start(bf16[2,180,512]{2,1,0:T(8,128)(2,1)S(1)} %reshape.1564), channel_id=1, source_target_pairs={{8,0},{16,8},{24,16},{9,1},{17,9},{25,17},{10,2},{18,10},{26,18},{... | collective-permute-start | bytes 1105928 | tf_op jit(solution)/shard_map/ppermute | solution.py:23
  184.9 21.1 %collective-permute-start.2 = (bf16[2,180,512]{2,1,0:T(8,128)(2,1)S(1)}, bf16[2,180,512]{2,1,0:T(8,128)(2,1)}, u32[]{:S(2)}, u32[]{:S(2)}) collective-permute-start(bf16[2,180,512]{2,1,0:T(8,128)(2,1)S(1)} %reshape.1564), channel_id=1, source_target_pairs={{0,8},{8,16},{16,24},{1,9},{9,17},{17,25},{2,10},{10,18},{18,26},{... | collective-permute-start | bytes 1105928 | tf_op jit(solution)/shard_map/ppermute | solution.py:20
  210.3 171.9 %all-to-all-start.2 = ((bf16[6,512,180]{2,0,1:T(8,128)(2,1)}), bf16[6,512,180]{2,0,1:T(8,128)(2,1)}, u32[]{:S(2)}, u32[]{:S(2)}) async-start(bf16[6,512,180]{2,0,1:T(8,128)(2,1)} %copy.380), calls=%async_computation.2 | async-start | bytes 4194304 | tf_op jit(solution)/shard_map/all_to_all | solution.py:129
  450.6 54.0 %all-to-all-start.3 = ((bf16[8,2,11520]{2,1,0:T(2,128)(2,1)}), bf16[8,2,11520]{2,1,0:T(2,128)(2,1)S(1)}, u32[]{:S(2)}, u32[]{:S(2)}) async-start(bf16[8,2,11520]{2,1,0:T(2,128)(2,1)} %reshape.1585), calls=%async_computation.3 | async-start | bytes 737280 | tf_op jit(solution)/shard_map/all_to_all | solution.py:136
  454.3 7.8 %copy-start.162 = (f32[2,64]{1,0:T(2,128)S(1)}, f32[2,64]{1,0:T(2,128)}, u32[]{:S(2)}) copy-start(f32[2,64]{1,0:T(2,128)} %get-tuple-element.265) | copy-start | bytes 1540
  454.3 7.8 %copy-start.158 = (f32[2,64]{1,0:T(2,128)S(1)}, f32[2,64]{1,0:T(2,128)}, u32[]{:S(2)}) copy-start(f32[2,64]{1,0:T(2,128)} %get-tuple-element.188) | copy-start | bytes 1540
  454.3 7.8 %copy-start.161 = (f32[2,64]{1,0:T(2,128)S(1)}, f32[2,64]{1,0:T(2,128)}, u32[]{:S(2)}) copy-start(f32[2,64]{1,0:T(2,128)} %get-tuple-element.226) | copy-start | bytes 1540
  454.3 7.8 %copy-start.160 = (f32[2,64]{1,0:T(2,128)S(1)}, f32[2,64]{1,0:T(2,128)}, u32[]{:S(2)}) copy-start(f32[2,64]{1,0:T(2,128)} %get-tuple-element.221) | copy-start | bytes 1540
  454.3 7.8 %copy-start.159 = (f32[2,64]{1,0:T(2,128)S(1)}, f32[2,64]{1,0:T(2,128)}, u32[]{:S(2)}) copy-start(f32[2,64]{1,0:T(2,128)} %get-tuple-element.163) | copy-start | bytes 1540
  454.4 7.9 %copy-start.157 = (f32[2,64]{1,0:T(2,128)S(1)}, f32[2,64]{1,0:T(2,128)}, u32[]{:S(2)}) copy-start(f32[2,64]{1,0:T(2,128)} %get-tuple-element.260) | copy-start | bytes 1540
  454.4 7.9 %copy-start.156 = (f32[2,64]{1,0:T(2,128)S(1)}, f32[2,64]{1,0:T(2,128)}, u32[]{:S(2)}) copy-start(f32[2,64]{1,0:T(2,128)} %get-tuple-element.268) | copy-start | bytes 1540
  454.4 7.9 %copy-start.155 = (f32[2,64]{1,0:T(2,128)S(1)}, f32[2,64]{1,0:T(2,128)}, u32[]{:S(2)}) copy-start(f32[2,64]{1,0:T(2,128)} %get-tuple-element.262) | copy-start | bytes 1540
  454.4 7.9 %copy-start.151 = (f32[2,64]{1,0:T(2,128)S(1)}, f32[2,64]{1,0:T(2,128)}, u32[]{:S(2)}) copy-start(f32[2,64]{1,0:T(2,128)} %get-tuple-element.185) | copy-start | bytes 1540
  454.4 8.0 %copy-start.154 = (f32[2,64]{1,0:T(2,128)S(1)}, f32[2,64]{1,0:T(2,128)}, u32[]{:S(2)}) copy-start(f32[2,64]{1,0:T(2,128)} %get-tuple-element.229) | copy-start | bytes 1540
  454.4 8.0 %copy-start.153 = (f32[2,64]{1,0:T(2,128)S(1)}, f32[2,64]{1,0:T(2,128)}, u32[]{:S(2)}) copy-start(f32[2,64]{1,0:T(2,128)} %get-tuple-element.224) | copy-start | bytes 1540
  454.4 8.0 %copy-start.152 = (f32[2,64]{1,0:T(2,128)S(1)}, f32[2,64]{1,0:T(2,128)}, u32[]{:S(2)}) copy-start(f32[2,64]{1,0:T(2,128)} %get-tuple-element.160) | copy-start | bytes 1540
  454.4 8.1 %copy-start.54 = (f32[2,5,8,13]{3,2,1,0:T(8,128)S(1)}, f32[2,5,8,13]{3,2,1,0:T(8,128)}, u32[]{:S(2)}) copy-start(f32[2,5,8,13]{3,2,1,0:T(8,128)} %param.27) | copy-start | bytes 12484
  (161 other events, 773.9 us)
Sparse Core Ops, SparseCore 0:
  203.3 173.8 all-reduce.3
where the time goes:
time: 522 us; the launch traced here: 516 us
  waiting for transfers between devices  157 us (30%)
  local copies, waits for them, and re-layouts  131 us (25%)
  blocking collectives  87.7 us (17%)
  other arithmetic  72.8 us (14%)
  starting transfers between devices  35.3 us (7%)
  between operations  17.5 us (3%)
  matrix products  14.1 us (3%)
    psum x1, waiting for transfers between devices, local(): lax.psum((grad_in_w, grad_out_w, partial_basis), ('lat', 'lon'))  136 us
    all_to_all x1, blocking collectives, local(): lax.all_to_all(terms, 'lon', split_axis=3, concat_axis=2, tiled=True)  46.7 us
    psum x1, blocking collectives, local(): lax.psum((grad_in_w, grad_out_w, partial_basis), ('lat', 'lon'))  40.9 us
    unnamed x443, local copies, waits for them, and re-layouts  30 us
    convert_element_type x14, local copies, waits for them, and re-layouts, local(): jnp.roll(cycle, -offset, axis=2).astype(jnp.float32)  24.1 us
    convert_element_type x1, other arithmetic, local(): back.astype(jnp.bfloat16)  20.4 us
    unnamed x4, other arithmetic  17.1 us
    slice x11, local copies, waits for them, and re-layouts, local(): grad_cycle[band_step:band_step + rows]  16.7 us
  transfers between devices with their start and end apart: 8, of which 4 were waited for; matrix products, arithmetic and copies ran while one was open for 11% of the time, Pallas kernels for 0%

commit v1 on v0

--- a/solution.py
+++ b/solution.py
@@ -1,8 +1,11 @@
+import functools
 import math
 
 import jax
 import jax.numpy as jnp
 from jax import lax
+from jax.experimental import pallas as pl
+from jax.experimental.pallas import tpu as pltpu
 from jax.sharding import PartitionSpec as P
 
 
@@ -146,6 +149,373 @@
     grad_fields = (grad_hidden.astype(jnp.float32) + back.astype(jnp.float32)).astype(jnp.bfloat16)
     return (result, grad_fields, total_in * factor, total_out * factor, total_basis * factor)
 
+MESH = pl.DeviceIdType.MESH
+TILE = 16
+GELU_SCALE = math.sqrt(2.0 / math.pi)
+GELU_CUBE = 0.044715
+
+
+def gelu_parts(x):
+    square = x * x
+    curve = jnp.tanh(GELU_SCALE * (x + GELU_CUBE * (square * x)))
+    half = 0.5 * (1.0 + curve)
+    slope = half + 0.5 * x * (1.0 - curve * curve) * (
+        GELU_SCALE * (1.0 + 3.0 * GELU_CUBE * square)
+    )
+    return x * half, slope
+
+
+def build_toeplitz(mask_ref, expand_ref, edge_ref, fwd_ref, bwd_ref, bands, count, basis_count):
+    reach = (count - 1) // 2
+    band_reach = (bands - 1) // 2
+    total = fwd_ref.shape[0]
+    span = 3 * TILE
+    depth = bands * span
+    lanes = expand_ref.shape[2]
+    rows = total * basis_count
+    coded = mask_ref[...].reshape(rows, mask_ref.shape[2]).astype(jnp.bfloat16)
+    lane = lax.broadcasted_iota(jnp.int32, (mask_ref.shape[2], lanes), 1)
+    source = lax.broadcasted_iota(jnp.int32, (mask_ref.shape[2], lanes), 0)
+    band_of = lane // span
+    live = lane < depth
+    row_lane = lax.broadcasted_iota(jnp.int32, (TILE, lanes), 1)
+    row_m = lax.broadcasted_iota(jnp.int32, (TILE, lanes), 0)
+    row_n = row_lane % span
+    for forward in (True, False):
+        slot = bands - 1 - band_of if forward else band_of
+        for tap in range(count):
+            pick = jnp.where(live & (source == tap * bands + slot), 1.0, 0.0).astype(jnp.bfloat16)
+            spread = jnp.dot(coded, pick, preferred_element_type=jnp.float32)
+            expand_ref[tap, band_reach * basis_count : band_reach * basis_count + rows] = spread
+        tap_of = (
+            row_n - row_m - TILE + reach if forward else row_m - row_n + TILE + reach
+        )
+        tap_of = jnp.where(row_lane < depth, tap_of, -1)
+        seg = lax.broadcasted_iota(jnp.int32, (basis_count, lanes), 1) // span
+
+        def one(i, carry):
+            acc = jnp.zeros((basis_count, TILE, lanes), jnp.float32)
+            for tap in range(count):
+                if forward:
+                    row = jnp.zeros((basis_count, lanes), jnp.float32)
+                    for step in range(bands):
+                        piece = expand_ref[
+                            tap,
+                            pl.ds(pl.multiple_of((i + step) * basis_count, basis_count), basis_count),
+                        ]
+                        row = jnp.where(seg == step, piece, row)
+                else:
+                    row = expand_ref[
+                        tap,
+                        pl.ds(
+                            pl.multiple_of((i + band_reach) * basis_count, basis_count), basis_count
+                        ),
+                    ]
+                acc = jnp.where((tap_of == tap)[None], row[:, None, :], acc)
+            out = acc.reshape(basis_count * TILE, lanes)[:, :depth].astype(jnp.bfloat16)
+            (fwd_ref if forward else bwd_ref)[i] = out
+            return carry
+
+        lax.fori_loop(0, total, one, 0)
+
+
+def block_kernel(
+    sizes,
+    f4,
+    c4,
+    mk,
+    basis,
+    w_in,
+    w_out,
+    res4,
+    gf4,
+    giw,
+    gow,
+    gb,
+    fx,
+    cx,
+    mx,
+    halo,
+    buf,
+    stage,
+    expand,
+    fwd,
+    bwd,
+    hx,
+    resx,
+    gx,
+    gfx,
+    mixed,
+    ghacc,
+    f_send,
+    f_recv,
+    c_send,
+    c_recv,
+    m_send,
+    m_recv,
+    h_send,
+    h_recv,
+    r_send,
+    r_recv,
+    g_send,
+    g_recv,
+):
+    lat_count, lon_count, rows, width, bands, count, basis_count, factor = sizes
+    band_reach = (bands - 1) // 2
+    total, padded_width, channels = fx.shape
+    pad = padded_width - width
+    blocks = padded_width // TILE
+    lat = lax.axis_index("lat")
+    lon = lax.axis_index("lon")
+    linear = lon * lat_count + lat
+    devices = lat_count * lon_count
+    after = lax.rem(linear + 1, devices)
+    before = lax.rem(linear + devices - 1, devices)
+    nxt = (lax.rem(after, lat_count), after // lat_count)
+    prv = (lax.rem(before, lat_count), before // lat_count)
+    peers = [(lax.rem(lat + off, lat_count), lon) for off in range(1, lat_count)]
+
+    barrier = pltpu.get_barrier_semaphore()
+    for who in peers + [nxt, prv]:
+        pl.semaphore_signal(barrier, inc=1, device_id=who, device_id_type=MESH)
+    pl.semaphore_wait(barrier, len(peers) + 2)
+
+    def remote(src, dst, send, recv, who):
+        copy = pltpu.make_async_remote_copy(
+            src_ref=src,
+            dst_ref=dst,
+            send_sem=send,
+            recv_sem=recv,
+            device_id=who,
+            device_id_type=MESH,
+        )
+        copy.start()
+        return copy
+
+    mine = pl.ds(lat * rows, rows)
+    f_copies = [
+        remote(f4.at[who[0]], fx.at[mine], f_send.at[n], f_recv.at[n], who)
+        for n, who in enumerate(peers)
+    ]
+    m_copies = [
+        remote(mk, mx.at[mine], m_send.at[n], m_recv.at[n], who) for n, who in enumerate(peers)
+    ]
+    c_copies = [
+        remote(c4.at[who[0]], cx.at[mine], c_send.at[n], c_recv.at[n], who)
+        for n, who in enumerate(peers)
+    ]
+    fx[mine] = f4[lat]
+    cx[mine] = c4[lat]
+    mx[mine] = mk[...]
+    buf[...] = jnp.zeros_like(buf)
+    stage[...] = jnp.zeros_like(stage)
+    expand[...] = jnp.zeros_like(expand)
+
+    def swap(own, which):
+        right = remote(
+            own.at[:, pl.ds(padded_width - TILE, TILE)],
+            halo.at[2 * which],
+            h_send.at[2 * which],
+            h_recv.at[2 * which],
+            nxt,
+        )
+        left = remote(
+            own.at[:, pl.ds(0, TILE)],
+            halo.at[2 * which + 1],
+            h_send.at[2 * which + 1],
+            h_recv.at[2 * which + 1],
+            prv,
+        )
+        return right, left
+
+    def fill(own, which):
+        stage[:, pad : pad + TILE] = halo[2 * which].astype(jnp.float32)
+        stage[:, TILE : TILE + padded_width] = own[...].astype(jnp.float32)
+        stage[:, TILE + width : 2 * TILE + width] = halo[2 * which + 1].astype(jnp.float32)
+        buf[band_reach : band_reach + total] = stage[...].astype(jnp.bfloat16)
+
+    for copy in m_copies:
+        copy.wait()
+    build_toeplitz(mx, expand, None, fwd, bwd, bands, count, basis_count)
+    for copy in f_copies:
+        copy.wait()
+    swaps = swap(fx, 0)
+    for copy in swaps:
+        copy.wait()
+    fill(fx, 0)
+
+    def view(i, b):
+        window = buf[pl.ds(i, bands), TILE * b : TILE * (b + 3), :]
+        return window.reshape(bands * 3 * TILE, channels)
+
+    weights = basis[...][:, None, :]
+
+    def conv_row(i, carry):
+        for b in range(blocks):
+            product = jnp.dot(fwd[i], view(i, b), preferred_element_type=jnp.float32)
+            conv = jnp.sum(product.reshape(basis_count, TILE, channels) * weights, axis=0)
+            here = slice(TILE * b, TILE * (b + 1))
+            hx[i, here] = (fx[i, here].astype(jnp.float32) + conv).astype(jnp.bfloat16)
+        return carry
+
+    lax.fori_loop(0, total, conv_row, 0)
+    for copy in c_copies:
+        copy.wait()
+
+    cells = total * padded_width
+    hidden = w_in.shape[1]
+    chunk = 256
+    mixed[...] = jnp.zeros_like(mixed)
+    ghacc[...] = jnp.zeros_like(ghacc)
+    leading = (((0,), (0,)), ((), ()))
+    trailing = (((1,), (1,)), ((), ()))
+
+    def mlp(step, carry):
+        part = pl.ds(pl.multiple_of(step * chunk, chunk), chunk)
+        flat = hx[...].reshape(cells, channels)
+        cot = cx[...].reshape(cells, channels)
+        w_up = w_in[:, part]
+        w_down = w_out[part, :]
+        pre = jnp.dot(flat, w_up, preferred_element_type=jnp.float32)
+        act, slope = gelu_parts(pre)
+        act = act.astype(jnp.bfloat16)
+        mixed[...] += jnp.dot(act, w_down, preferred_element_type=jnp.float32)
+        gow[part, :] = factor * lax.dot_general(
+            act, cot, leading, preferred_element_type=jnp.float32
+        )
+        grad_act = lax.dot_general(cot, w_down, trailing, preferred_element_type=jnp.float32)
+        grad_pre = (grad_act * slope).astype(jnp.bfloat16)
+        giw[:, part] = factor * lax.dot_general(
+            flat, grad_pre, leading, preferred_element_type=jnp.float32
+        )
+        ghacc[...] += lax.dot_general(grad_pre, w_up, trailing, preferred_element_type=jnp.float32)
+        return carry
+
+    lax.fori_loop(0, hidden // chunk, mlp, 0)
+    shape = (total, padded_width, channels)
+    gx[...] = (cx[...].astype(jnp.float32) + ghacc[...].reshape(shape)).astype(jnp.bfloat16)
+    swaps = swap(gx, 1)
+    resx[...] = (hx[...].astype(jnp.float32) + mixed[...].reshape(shape)).astype(jnp.bfloat16)
+    r_copies = [
+        remote(
+            resx.at[pl.ds(who[0] * rows, rows)], res4.at[lat], r_send.at[n], r_recv.at[n], who
+        )
+        for n, who in enumerate(peers)
+    ]
+    res4[lat] = resx[mine]
+    for copy in swaps:
+        copy.wait()
+    fill(gx, 1)
+
+    def back_row(i, carry):
+        for b in range(blocks):
+            product = jnp.dot(bwd[i], view(i, b), preferred_element_type=jnp.float32).reshape(
+                basis_count, TILE, channels
+            )
+            here = slice(TILE * b, TILE * (b + 1))
+            back = jnp.sum(product * weights, axis=0).astype(jnp.bfloat16).astype(jnp.float32)
+            gfx[i, here] = (gx[i, here].astype(jnp.float32) + back).astype(jnp.bfloat16)
+            field = fx[i, here].astype(jnp.float32)
+            carry = carry + jnp.sum(product * field[None], axis=1)
+        return carry
+
+    gb[...] = factor * lax.fori_loop(
+        0, total, back_row, jnp.zeros((basis_count, channels), jnp.float32)
+    )
+    g_copies = [
+        remote(gfx.at[pl.ds(who[0] * rows, rows)], gf4.at[lat], g_send.at[n], g_recv.at[n], who)
+        for n, who in enumerate(peers)
+    ]
+    gf4[lat] = gfx[mine]
+    for copy in r_copies + g_copies:
+        copy.wait()
+
+
+def fused(fields_in, span, filters, basis, w_in, w_out, cotangent):
+    rows, width, channels = fields_in.shape
+    lat_count = lax.axis_size("lat")
+    lon_count = lax.axis_size("lon")
+    part = width // lat_count
+    padded_part = -(-part // TILE) * TILE
+    total = rows * lat_count
+    bands, basis_count, count = filters.shape[1:]
+    band_reach = (bands - 1) // 2
+    hidden = w_in.shape[1]
+    factor = 1.0 / math.sqrt(total * lon_count * width)
+    masked = tap_mask(filters, span)
+    coded = jnp.transpose(masked, (0, 2, 3, 1)).reshape(rows, basis_count, count * bands)
+    coded = jnp.pad(coded, ((0, 0), (0, 0), (0, 128 - count * bands)))
+
+    def split(block):
+        cut = block.reshape(rows, lat_count, part, channels).swapaxes(0, 1)
+        return jnp.pad(cut, ((0, 0), (0, 0), (0, padded_part - part), (0, 0)))
+
+    def joined(block):
+        return block[:, :, :part].swapaxes(0, 1).reshape(rows, width, channels)
+
+    bf16 = jnp.bfloat16
+    f32 = jnp.float32
+    window = padded_part + 2 * TILE
+    lanes = -(-bands * 3 * TILE // 128) * 128
+    cell_shape = (total, padded_part, channels)
+    dma = pltpu.SemaphoreType.DMA
+    others = lat_count - 1
+    sizes = (lat_count, lon_count, rows, part, bands, count, basis_count, factor)
+    vmem = pl.BlockSpec(memory_space=pltpu.VMEM)
+    out = pl.pallas_call(
+        functools.partial(block_kernel, sizes),
+        out_shape=(
+            jax.ShapeDtypeStruct((lat_count, rows, padded_part, channels), bf16),
+            jax.ShapeDtypeStruct((lat_count, rows, padded_part, channels), bf16),
+            jax.ShapeDtypeStruct((channels, hidden), f32),
+            jax.ShapeDtypeStruct((hidden, channels), f32),
+            jax.ShapeDtypeStruct((basis_count, channels), f32),
+        ),
+        in_specs=[vmem] * 6,
+        out_specs=[vmem] * 5,
+        scratch_shapes=[
+            pltpu.VMEM(cell_shape, bf16),
+            pltpu.VMEM(cell_shape, bf16),
+            pltpu.VMEM((total, basis_count, 128), f32),
+            pltpu.VMEM((4, total, TILE, channels), bf16),
+            pltpu.VMEM((total + 2 * band_reach, window, channels), bf16),
+            pltpu.VMEM((total, window, channels), f32),
+            pltpu.VMEM((count, (total + 2 * band_reach) * basis_count, lanes), f32),
+            pltpu.VMEM((total, basis_count * TILE, bands * 3 * TILE), bf16),
+            pltpu.VMEM((total, basis_count * TILE, bands * 3 * TILE), bf16),
+            pltpu.VMEM(cell_shape, bf16),
+            pltpu.VMEM(cell_shape, bf16),
+            pltpu.VMEM(cell_shape, bf16),
+            pltpu.VMEM(cell_shape, bf16),
+            pltpu.VMEM((total * padded_part, channels), f32),
+            pltpu.VMEM((total * padded_part, channels), f32),
+            dma((others,)),
+            dma((others,)),
+            dma((others,)),
+            dma((others,)),
+            dma((others,)),
+            dma((others,)),
+            dma((4,)),
+            dma((4,)),
+            dma((others,)),
+            dma((others,)),
+            dma((others,)),
+            dma((others,)),
+        ],
+        compiler_params=pltpu.CompilerParams(
+            collective_id=0, has_side_effects=True, vmem_limit_bytes=52 * 2**20
+        ),
+    )(split(fields_in), split(cotangent), coded, basis, w_in, w_out)
+    result, grad_fields, grad_in, grad_out, grad_basis = out
+    totals = lax.psum((grad_in, grad_out, grad_basis), ("lat", "lon"))
+    return (joined(result), joined(grad_fields)) + totals
+
+
+def fits(mesh, fields_shape):
+    lat_count, lon_count = mesh.shape["lat"], mesh.shape["lon"]
+    share, left = divmod(fields_shape[1], lat_count * lon_count)
+    return left == 0 and share >= TILE and lat_count > 1 and (-share) % TILE <= TILE - 6
+
 
 def solution(mesh):
     in_specs = (
@@ -158,4 +528,11 @@
         P("lat", "lon", None),
     )
     out_specs = (P("lat", "lon", None), P("lat", "lon", None), P(), P(), P())
-    return jax.shard_map(local, mesh=mesh, in_specs=in_specs, out_specs=out_specs, check_vma=False)
+
+    def run(fields_in, *rest):
+        body = fused if fits(mesh, fields_in.shape) else local
+        return jax.shard_map(
+            body, mesh=mesh, in_specs=in_specs, out_specs=out_specs, check_vma=False
+        )(fields_in, *rest)
+
+    return run

time: 522 us -> 215 us (0.41); the launches traced: 516 us -> 215 us
  local copies, waits for them, and re-layouts: 131 us -> 9.31 us
  other arithmetic: 72.8 us -> 0.08 us
  waiting for transfers between devices: 157 us -> 101 us
  Pallas kernels: 0 us -> 50.2 us
  blocking collectives: 87.7 us -> 40.2 us
  starting transfers between devices: 35.3 us -> 0.04 us
  matrix products: 14.1 us -> 0 us
    pallas_call x0 -> x1, Pallas kernels: none -> 50.2 us  [fused(): pl.pallas_call(functools.partial(block_kernel, sizes), out_shape=(jax.Sha...]
    all_to_all x1 -> x0, blocking collectives: 46.7 us -> none  [local(): lax.all_to_all(terms, 'lon', split_axis=3, concat_axis=2, tiled=True)]
    slice x61 -> x0, local copies, waits for them, and re-layouts: 46.4 us -> none  [the longest x11 16.7 us: local(): grad_cycle[band_step:band_step + rows]]
    psum x1, waiting for transfers between devices: 136 us -> 101 us  [fused(): totals = lax.psum((grad_in, grad_out, grad_basis), ('lat', 'lon'))]
    convert_element_type x11 -> x0, other arithmetic: 29.2 us -> none  [the longest x1 20.4 us: local(): back.astype(jnp.bfloat16)]
    convert_element_type x19 -> x0, local copies, waits for them, and re-layouts: 28.2 us -> none  [the longest x14 24.1 us: local(): jnp.roll(cycle, -offset, axis=2).astype(jnp.float32)]
    unnamed x443 -> x10, local copies, waits for them, and re-layouts: 30 us -> 4.64 us
    ppermute x4 -> x0, starting transfers between devices: 21 us -> none  [the longest x1 12.9 us: padded(): lax.ppermute(lax.slice_in_dim(block, block.shape[dim] - width, None, axis...]
  transfers between devices with their start and end apart: 8 -> 1, of which waited for: 4 -> 1; matrix products, arithmetic and copies ran while one was open for 11% -> 1% of each run, Pallas kernels for 0% -> 0%
where the time goes in v1:
time: 215 us
  waiting for transfers between devices  101 us (47%)
  Pallas kernels  50.2 us (23%)
  blocking collectives  40.2 us (19%)
  between operations  14.1 us (7%)
  local copies, waits for them, and re-layouts  9.31 us (4%)
    psum x1, waiting for transfers between devices, fused(): totals = lax.psum((grad_in, grad_out, grad_basis), ('lat', 'lon'))  101 us
    pallas_call x1, Pallas kernels, fused(): pl.pallas_call(functools.partial(block_kernel, sizes), out_shape=(jax.Sha...  50.2 us
    psum x1, blocking collectives, fused(): totals = lax.psum((grad_in, grad_out, grad_basis), ('lat', 'lon'))  40.2 us
    unnamed x10, local copies, waits for them, and re-layouts  4.64 us
  transfers between devices with their start and end apart: 1, of which 1 were waited for; matrix products, arithmetic and copies ran while one was open for 1% of the time, Pallas kernels for 0%

profile of v1, /device:TPU:0, one launch (start us, length us, event | category | flops | bytes accessed | tf_op | source)
XLA Modules:
  0.0 214.6 jit_solution(4088051002809318572)
XLA Ops:
  7.2 0.0 copy-start.3
  7.2 0.0 copy-start.2
  7.2 0.0 copy-start
  7.2 0.0 all-reduce.6.cloned.1.call-start
  7.3 1.0 copy.22
  8.3 1.0 copy.21
  9.4 0.0 copy-done.3
  9.4 0.1 compare_convert_fusion
  9.5 0.0 copy-done.2
  9.5 0.1 copy.15
  9.7 0.1 copy.16
  9.7 0.0 copy-done
  9.7 50.2 %shard_map.110 = (bf16[4,2,48,512]{3,2,1,0:T(8,128)(2,1)S(1)}, bf16[4,2,48,512]{3,2,1,0:T(8,128)(2,1)S(1)}, f32[512,1024]{1,0:T(8,128)}, f32[1024,512]{1,0:T(8,128)}, f32[8,512]{1,0:T(8,128)S(1)}) custom-call(bf16[4,2,48,512]{3,2,1,0:T(8,128)(2,1)S(1)} %pad.11.f4, bf16[4,2,48,512]{3,2,1,0:T(8,128)(2,1)S(1)} %pad.12.c4, f32[2,8,128]{2,1,0:T(8,128)S(1)} %pad.13.mk, ...), custom_call_target="tpu_custom_call" | custom-call | tf_op jit(solution)/shard_map/pallas_call | solution.py:465
  60.0 0.0 all-reduce.6.cloned.1.call-update
  60.0 0.1 slice_bitcast_fusion
  60.1 1.1 copy.17
  61.2 1.1 copy.18
  62.3 40.2 %psum.23 = f32[8,512]{1,0:T(8,128)} all-reduce(f32[8,512]{1,0:T(8,128)S(1)} %get-tuple-element.14), channel_id=1, replica_groups=mesh['lat'=4,'lon'=8] {'lat','lon'}, use_global_device_ids=true, to_apply=%region_2.3 | all-reduce | flops 4096 | bytes 32768 | tf_op jit(solution)/shard_map/psum | solution.py:510
  102.5 100.6 %all-reduce.6.cloned.1.call-done = (f32[512,1024]{1,0:T(8,128)}, f32[1024,512]{1,0:T(8,128)}) async-done(((f32[512,1024]{1,0:T(8,128)}, f32[1024,512]{1,0:T(8,128)}), (f32[512,1024]{1,0:T(8,128)}, f32[1024,512]{1,0:T(8,128)})) %all-reduce.6.cloned.1.call-update) | async-done | bytes 4194320 | tf_op jit(solution)/shard_map/psum | solution.py:510
  203.1 0.0 copy-start.1
  203.1 3.3 %copy.27 = f32[512,1024]{1,0:T(8,128)} copy(f32[512,1024]{1,0:T(8,128)} %get-tuple-element.26) | data formatting | bytes 4194304
  206.4 0.0 copy-done.1
  206.4 1.3 copy.28
  (5 shorter events, 0.1 us)
Async XLA Ops:
  7.2 2.2 %copy-start.3 = (s32[2,5]{1,0:T(2,128)S(1)}, s32[2,5]{1,0:T(2,128)}, u32[]{:S(2)}) copy-start(s32[2,5]{1,0:T(2,128)} %param.8) | copy-start | bytes 124
  7.2 2.3 %copy-start.2 = (f32[2,5,8,13]{3,2,1,0:T(8,128)S(1)}, f32[2,5,8,13]{3,2,1,0:T(8,128)}, u32[]{:S(2)}) copy-start(f32[2,5,8,13]{3,2,1,0:T(8,128)} %param.9) | copy-start | bytes 12484
  7.2 2.6 %copy-start = (f32[8,512]{1,0:T(8,128)S(1)}, f32[8,512]{1,0:T(8,128)}, u32[]{:S(2)}) copy-start(f32[8,512]{1,0:T(8,128)} %basis.1) | copy-start | bytes 49156
  7.2 195.9 %all-reduce.6.cloned.1.call-start = ((), (), s32[]{:S(2)}) async-start(), calls=%async_computation | async-start | bytes 8388608 | tf_op jit(solution)/shard_map/psum | solution.py:510
  203.1 3.3 %copy-start.1 = (f32[1024,512]{1,0:T(8,128)S(1)}, f32[1024,512]{1,0:T(8,128)}, u32[]{:S(2)}) copy-start(f32[1024,512]{1,0:T(8,128)} %get-tuple-element.27) | copy-start | bytes 6291460
Sparse Core Ops, SparseCore 0:
  60.1 142.9 all-reduce.5

commit v2 on v1

--- a/solution.py
+++ b/solution.py
@@ -151,6 +151,7 @@
 
 MESH = pl.DeviceIdType.MESH
 TILE = 16
+CHUNK = 256
 GELU_SCALE = math.sqrt(2.0 / math.pi)
 GELU_CUBE = 0.044715
 
@@ -165,7 +166,7 @@
     return x * half, slope
 
 
-def build_toeplitz(mask_ref, expand_ref, edge_ref, fwd_ref, bwd_ref, bands, count, basis_count):
+def build_toeplitz(mask_ref, expand_ref, fwd_ref, bwd_ref, bands, count, basis_count):
     reach = (count - 1) // 2
     band_reach = (bands - 1) // 2
     total = fwd_ref.shape[0]
@@ -229,8 +230,7 @@
     w_out,
     res4,
     gf4,
-    giw,
-    gow,
+    gw,
     gb,
     fx,
     cx,
@@ -247,6 +247,16 @@
     gfx,
     mixed,
     ghacc,
+    part_w,
+    core_in,
+    core_sum,
+    lat_in,
+    lat_sum,
+    z_in,
+    gb_part,
+    gb_core,
+    gb_lat,
+    gb_z,
     f_send,
     f_recv,
     c_send,
@@ -259,6 +269,20 @@
     r_recv,
     g_send,
     g_recv,
+    p_send,
+    p_recv,
+    l_send,
+    l_recv,
+    z_send,
+    z_recv,
+    zg_send,
+    zg_recv,
+    lg_send,
+    lg_recv,
+    pg_send,
+    pg_recv,
+    b_send,
+    b_recv,
 ):
     lat_count, lon_count, rows, width, bands, count, basis_count, factor = sizes
     band_reach = (bands - 1) // 2
@@ -274,11 +298,19 @@
     nxt = (lax.rem(after, lat_count), after // lat_count)
     prv = (lax.rem(before, lat_count), before // lat_count)
     peers = [(lax.rem(lat + off, lat_count), lon) for off in range(1, lat_count)]
+    z_count = lon_count // 2
+    core = lax.rem(lon, 2)
+    zpos = lon // 2
+    sibling = (lat, lon + 1 - 2 * core)
+    z_peers = [
+        (lat, 2 * lax.rem(zpos + off, z_count) + core) for off in range(1, z_count)
+    ]
+    greeted = peers + [nxt, prv, sibling] + z_peers
 
     barrier = pltpu.get_barrier_semaphore()
-    for who in peers + [nxt, prv]:
+    for who in greeted:
         pl.semaphore_signal(barrier, inc=1, device_id=who, device_id_type=MESH)
-    pl.semaphore_wait(barrier, len(peers) + 2)
+    pl.semaphore_wait(barrier, len(greeted))
 
     def remote(src, dst, send, recv, who):
         copy = pltpu.make_async_remote_copy(
@@ -336,7 +368,7 @@
 
     for copy in m_copies:
         copy.wait()
-    build_toeplitz(mx, expand, None, fwd, bwd, bands, count, basis_count)
+    build_toeplitz(mx, expand, fwd, bwd, bands, count, basis_count)
     for copy in f_copies:
         copy.wait()
     swaps = swap(fx, 0)
@@ -364,14 +396,105 @@
 
     cells = total * padded_width
     hidden = w_in.shape[1]
-    chunk = 256
+    chunk = CHUNK
     mixed[...] = jnp.zeros_like(mixed)
     ghacc[...] = jnp.zeros_like(ghacc)
     leading = (((0,), (0,)), ((), ()))
     trailing = (((1,), (1,)), ((), ()))
 
-    def mlp(step, carry):
-        part = pl.ds(pl.multiple_of(step * chunk, chunk), chunk)
+    steps = hidden // chunk
+    core_rows = part_w.shape[1] // 2
+    lat_rows = core_rows // lat_count
+    z_rows = lat_rows // z_count
+    f32 = jnp.float32
+
+    def rows_at(start, size):
+        return pl.ds(pl.multiple_of(start, TILE), size)
+
+    core_block = rows_at(core * core_rows, core_rows)
+    lat_block = rows_at(core * core_rows + lat * lat_rows, lat_rows)
+    z_block = rows_at(core * core_rows + lat * lat_rows + zpos * z_rows, z_rows)
+
+    def wait(copies):
+        for copy in copies:
+            copy.wait()
+
+    def send_core(c):
+        other = rows_at((1 - core) * core_rows, core_rows)
+        return [
+            remote(part_w.at[c, other], core_in.at[c], p_send.at[c], p_recv.at[c], sibling)
+        ]
+
+    def send_lat(c):
+        core_sum[c] = (part_w[c, core_block].astype(f32) + core_in[c].astype(f32)).astype(
+            jnp.bfloat16
+        )
+        return [
+            remote(
+                core_sum.at[c, rows_at(who[0] * lat_rows, lat_rows)],
+                lat_in.at[c, n],
+                l_send.at[c, n],
+                l_recv.at[c, n],
+                who,
+            )
+            for n, who in enumerate(peers)
+        ]
+
+    def send_z(c):
+        value = core_sum[c, rows_at(lat * lat_rows, lat_rows)].astype(f32)
+        for n in range(len(peers)):
+            value = value + lat_in[c, n].astype(f32)
+        lat_sum[c] = value.astype(jnp.bfloat16)
+        return [
+            remote(
+                lat_sum.at[c, rows_at((who[1] // 2) * z_rows, z_rows)],
+                z_in.at[c, n],
+                z_send.at[c, n],
+                z_recv.at[c, n],
+                who,
+            )
+            for n, who in enumerate(z_peers)
+        ]
+
+    def share_z(c):
+        value = lat_sum[c, rows_at(zpos * z_rows, z_rows)].astype(f32)
+        for n in range(len(z_peers)):
+            value = value + z_in[c, n].astype(f32)
+        gw[c, z_block] = value.astype(jnp.bfloat16)
+        return [
+            remote(
+                gw.at[c, z_block], gw.at[c, z_block], zg_send.at[c, n], zg_recv.at[c, n], who
+            )
+            for n, who in enumerate(z_peers)
+        ]
+
+    def share_lat(c):
+        return [
+            remote(
+                gw.at[c, lat_block], gw.at[c, lat_block], lg_send.at[c, n], lg_recv.at[c, n], who
+            )
+            for n, who in enumerate(peers)
+        ]
+
+    def share_core(c):
+        return [
+            remote(gw.at[c, core_block], gw.at[c, core_block], pg_send.at[c], pg_recv.at[c], sibling)
+        ]
+
+    stages = (send_core, send_lat, send_z, share_z, share_lat, share_core)
+    flight = {}
+    reached = [0] * steps
+
+    def advance(c):
+        level = reached[c]
+        if level > 0:
+            wait(flight[c])
+        if level < len(stages):
+            flight[c] = stages[level](c)
+        reached[c] = level + 1
+
+    def mlp(step):
+        part = pl.ds(step * chunk, chunk)
         flat = hx[...].reshape(cells, channels)
         cot = cx[...].reshape(cells, channels)
         w_up = w_in[:, part]
@@ -380,18 +503,23 @@
         act, slope = gelu_parts(pre)
         act = act.astype(jnp.bfloat16)
         mixed[...] += jnp.dot(act, w_down, preferred_element_type=jnp.float32)
-        gow[part, :] = factor * lax.dot_general(
-            act, cot, leading, preferred_element_type=jnp.float32
-        )
+        grad_down = lax.dot_general(act, cot, leading, preferred_element_type=jnp.float32)
+        part_w[step, :chunk] = (factor * grad_down).astype(jnp.bfloat16)
         grad_act = lax.dot_general(cot, w_down, trailing, preferred_element_type=jnp.float32)
         grad_pre = (grad_act * slope).astype(jnp.bfloat16)
-        giw[:, part] = factor * lax.dot_general(
-            flat, grad_pre, leading, preferred_element_type=jnp.float32
-        )
+        grad_up = lax.dot_general(flat, grad_pre, leading, preferred_element_type=jnp.float32)
+        grad_up = (factor * grad_up).astype(jnp.bfloat16)
+        for cut in range(channels // chunk):
+            part_w[step, chunk:, cut * chunk : (cut + 1) * chunk] = grad_up[
+                cut * chunk : (cut + 1) * chunk
+            ]
         ghacc[...] += lax.dot_general(grad_pre, w_up, trailing, preferred_element_type=jnp.float32)
-        return carry
-
-    lax.fori_loop(0, hidden // chunk, mlp, 0)
+
+    for step in range(steps):
+        mlp(step)
+        advance(step)
+        if step > 0:
+            advance(step - 1)
     shape = (total, padded_width, channels)
     gx[...] = (cx[...].astype(jnp.float32) + ghacc[...].reshape(shape)).astype(jnp.bfloat16)
     swaps = swap(gx, 1)
@@ -403,6 +531,8 @@
         for n, who in enumerate(peers)
     ]
     res4[lat] = resx[mine]
+    advance(steps - 1)
+    advance(0)
     for copy in swaps:
         copy.wait()
     fill(gx, 1)
@@ -419,16 +549,51 @@
             carry = carry + jnp.sum(product * field[None], axis=1)
         return carry
 
-    gb[...] = factor * lax.fori_loop(
-        0, total, back_row, jnp.zeros((basis_count, channels), jnp.float32)
-    )
+    grad_basis = jnp.zeros((basis_count, channels), jnp.float32)
+    quarter = total // 4
+    for turn in range(4):
+        grad_basis = lax.fori_loop(quarter * turn, quarter * (turn + 1), back_row, grad_basis)
+        for c in range(min(turn + 1, steps - 1) , -1, -1):
+            if reached[c] < turn + 4 - c:
+                advance(c)
+    gb_part[...] = factor * grad_basis
     g_copies = [
         remote(gfx.at[pl.ds(who[0] * rows, rows)], gf4.at[lat], g_send.at[n], g_recv.at[n], who)
         for n, who in enumerate(peers)
     ]
     gf4[lat] = gfx[mine]
-    for copy in r_copies + g_copies:
-        copy.wait()
+    b_copies = [remote(gb_part, gb_core, b_send.at[0], b_recv.at[0], sibling)]
+
+    def catch_up(level):
+        for c in range(steps):
+            while reached[c] < level:
+                advance(c)
+
+    catch_up(4)
+    wait(b_copies)
+    gb_lat[lat] = gb_part[...] + gb_core[...]
+    b_copies = [
+        remote(gb_lat.at[lat], gb_lat.at[lat], b_send.at[1 + n], b_recv.at[1 + n], who)
+        for n, who in enumerate(peers)
+    ]
+    catch_up(5)
+    wait(b_copies)
+    gb_z[zpos] = jnp.sum(gb_lat[...], axis=0)
+    b_copies = [
+        remote(
+            gb_z.at[zpos],
+            gb_z.at[zpos],
+            b_send.at[lat_count + n],
+            b_recv.at[lat_count + n],
+            who,
+        )
+        for n, who in enumerate(z_peers)
+    ]
+    catch_up(6)
+    wait(b_copies)
+    gb[...] = jnp.sum(gb_z[...], axis=0)
+    catch_up(7)
+    wait(r_copies + g_copies)
 
 
 def fused(fields_in, span, filters, basis, w_in, w_out, cotangent):
@@ -459,6 +624,10 @@
     lanes = -(-bands * 3 * TILE // 128) * 128
     cell_shape = (total, padded_part, channels)
     dma = pltpu.SemaphoreType.DMA
+    z_count = lon_count // 2
+    steps = hidden // CHUNK
+    piece = 2 * CHUNK
+    lat_piece = piece // (2 * lat_count)
     others = lat_count - 1
     sizes = (lat_count, lon_count, rows, part, bands, count, basis_count, factor)
     vmem = pl.BlockSpec(memory_space=pltpu.VMEM)
@@ -467,12 +636,11 @@
         out_shape=(
             jax.ShapeDtypeStruct((lat_count, rows, padded_part, channels), bf16),
             jax.ShapeDtypeStruct((lat_count, rows, padded_part, channels), bf16),
-            jax.ShapeDtypeStruct((channels, hidden), f32),
-            jax.ShapeDtypeStruct((hidden, channels), f32),
+            jax.ShapeDtypeStruct((steps, piece, channels), bf16),
             jax.ShapeDtypeStruct((basis_count, channels), f32),
         ),
         in_specs=[vmem] * 6,
-        out_specs=[vmem] * 5,
+        out_specs=[vmem] * 4,
         scratch_shapes=[
             pltpu.VMEM(cell_shape, bf16),
             pltpu.VMEM(cell_shape, bf16),
@@ -489,6 +657,16 @@
             pltpu.VMEM(cell_shape, bf16),
             pltpu.VMEM((total * padded_part, channels), f32),
             pltpu.VMEM((total * padded_part, channels), f32),
+            pltpu.VMEM((steps, piece, channels), bf16),
+            pltpu.VMEM((steps, piece // 2, channels), bf16),
+            pltpu.VMEM((steps, piece // 2, channels), bf16),
+            pltpu.VMEM((steps, others, lat_piece, channels), bf16),
+            pltpu.VMEM((steps, lat_piece, channels), bf16),
+            pltpu.VMEM((steps, z_count - 1, lat_piece // z_count, channels), bf16),
+            pltpu.VMEM((basis_count, channels), f32),
+            pltpu.VMEM((basis_count, channels), f32),
+            pltpu.VMEM((lat_count, basis_count, channels), f32),
+            pltpu.VMEM((z_count, basis_count, channels), f32),
             dma((others,)),
             dma((others,)),
             dma((others,)),
@@ -501,20 +679,39 @@
             dma((others,)),
             dma((others,)),
             dma((others,)),
+            dma((steps,)),
+            dma((steps,)),
+            dma((steps, others)),
+            dma((steps, others)),
+            dma((steps, z_count - 1)),
+            dma((steps, z_count - 1)),
+            dma((steps, z_count - 1)),
+            dma((steps, z_count - 1)),
+            dma((steps, others)),
+            dma((steps, others)),
+            dma((steps,)),
+            dma((steps,)),
+            dma((lat_count + z_count - 1,)),
+            dma((lat_count + z_count - 1,)),
         ],
         compiler_params=pltpu.CompilerParams(
             collective_id=0, has_side_effects=True, vmem_limit_bytes=52 * 2**20
         ),
     )(split(fields_in), split(cotangent), coded, basis, w_in, w_out)
-    result, grad_fields, grad_in, grad_out, grad_basis = out
-    totals = lax.psum((grad_in, grad_out, grad_basis), ("lat", "lon"))
-    return (joined(result), joined(grad_fields)) + totals
+    result, grad_fields, grads, grad_basis = out
+    grad_out = grads[:, :CHUNK].reshape(hidden, channels).astype(f32)
+    grad_in = grads[:, CHUNK:].reshape(steps, CHUNK, channels // CHUNK, CHUNK)
+    grad_in = grad_in.transpose(2, 1, 0, 3).reshape(channels, hidden).astype(f32)
+    return (joined(result), joined(grad_fields), grad_in, grad_out, grad_basis)
 
 
 def fits(mesh, fields_shape):
     lat_count, lon_count = mesh.shape["lat"], mesh.shape["lon"]
     share, left = divmod(fields_shape[1], lat_count * lon_count)
-    return left == 0 and share >= TILE and lat_count > 1 and (-share) % TILE <= TILE - 6
+    pieces = CHUNK % (lat_count * max(1, lon_count // 2) * TILE) == 0
+    even = lon_count % 2 == 0 and lon_count > 2 and fields_shape[0] % 4 == 0
+    wide = left == 0 and share >= TILE and (-share) % TILE <= TILE - 6
+    return pieces and even and wide and lat_count > 1
 
 
 def solution(mesh):

time: 215 us -> 91.3 us (0.42)
  waiting for transfers between devices: 101 us -> 0 us
  blocking collectives: 40.2 us -> 0 us
  Pallas kernels: 50.2 us -> 75.9 us
  between operations: 14.1 us -> 0.74 us
  local copies, waits for them, and re-layouts: 9.31 us -> 12.4 us
    psum x1 -> x0, waiting for transfers between devices: 101 us -> none  [fused(): totals = lax.psum((grad_in, grad_out, grad_basis), ('lat', 'lon'))]
    psum x1 -> x0, blocking collectives: 40.2 us -> none  [fused(): totals = lax.psum((grad_in, grad_out, grad_basis), ('lat', 'lon'))]
    pallas_call x1, Pallas kernels: 50.2 us -> 75.9 us  [fused(): pl.pallas_call(functools.partial(block_kernel, sizes), out_shape=(jax.Sha...]
    convert_element_type x0 -> x2, local copies, waits for them, and re-layouts: none -> 5.29 us  [fused(): grad_in.transpose(2, 1, 0, 3).reshape(channels, hidden).astype(f32)]
    unnamed x10, local copies, waits for them, and re-layouts: 4.64 us -> 2.4 us
  transfers between devices with their start and end apart: 1 -> 0, of which waited for: 1 -> 0; matrix products, arithmetic and copies ran while one was open for 1% -> 0% of each run, Pallas kernels for 0% -> 0%
where the time goes in v2:
time: 91.3 us; the launch traced here: 91.1 us
  Pallas kernels  75.9 us (83%)
  local copies, waits for them, and re-layouts  12.4 us (14%)
  other arithmetic  2.11 us (2%)
    pallas_call x1, Pallas kernels, fused(): pl.pallas_call(functools.partial(block_kernel, sizes), out_shape=(jax.Sha...  75.9 us
    convert_element_type x2, local copies, waits for them, and re-layouts, fused(): grad_in.transpose(2, 1, 0, 3).reshape(channels, hidden).astype(f32)  5.29 us
    unnamed x10, local copies, waits for them, and re-layouts  2.4 us
    transpose x3, local copies, waits for them, and re-layouts, joined(): return block[:, :, :part].swapaxes(0, 1).reshape(rows, width, channels)  2.3 us
    reshape x2, local copies, waits for them, and re-layouts, split(): cut = block.reshape(rows, lat_count, part, channels).swapaxes(0, 1)  2.08 us

profile of v2, /device:TPU:0, one launch (start us, length us, event | category | flops | bytes accessed | tf_op | source)
XLA Modules:
  0.0 91.1 jit_solution(13271753288095788568)
XLA Ops:
  0.6 0.0 copy-start.3
  0.6 0.0 copy-start.2
  0.7 0.0 copy-start
  0.7 1.1 %copy.25 = bf16[2,4,45,512]{3,2,0,1:T(8,128)(2,1)S(1)} copy(bf16[2,4,45,512]{3,0,2,1:T(2,128)(2,1)} %bitcast.29) | data formatting | bytes 737280 | tf_op jit(solution)/shard_map/reshape | solution.py:615
  1.8 1.0 %copy.24 = bf16[2,4,45,512]{3,2,0,1:T(8,128)(2,1)S(1)} copy(bf16[2,4,45,512]{3,0,2,1:T(2,128)(2,1)} %bitcast.30) | data formatting | bytes 737280 | tf_op jit(solution)/shard_map/reshape | solution.py:615
  2.9 0.0 copy-done.3
  2.9 0.1 compare_convert_fusion
  2.9 0.0 copy-done.2
  2.9 0.1 copy.16
  3.1 0.1 copy.17
  3.2 0.0 copy-done
  3.2 75.9 %shard_map.110 = (bf16[4,2,48,512]{3,2,1,0:T(8,128)(2,1)S(1)}, bf16[4,2,48,512]{3,2,1,0:T(8,128)(2,1)S(1)}, bf16[4,512,512]{2,1,0:T(8,128)(2,1)}, f32[8,512]{1,0:T(8,128)S(1)}) custom-call(bf16[4,2,48,512]{3,2,1,0:T(8,128)(2,1)S(1)} %pad.11.f4, bf16[4,2,48,512]{3,2,1,0:T(8,128)(2,1)S(1)} %pad.12.c4, f32[2,8,128]{2,1,0:T(8,128)S(1)} %pad.13.mk, ...), custom_call_target="tpu_custom_call" | custom-call | tf_op jit(solution)/shard_map/pallas_call | solution.py:634
  79.0 0.0 copy-start.1
  79.0 0.1 slice_bitcast_fusion
  79.1 1.1 %copy.18 = bf16[2,4,45,512]{3,0,2,1:T(2,128)(2,1)} copy(bf16[2,4,45,512]{3,2,0,1:T(8,128)(2,1)S(1)} %get-tuple-element.16) | data formatting | bytes 737280 | tf_op jit(solution)/shard_map/transpose | solution.py:619
  80.2 1.1 %copy.19 = bf16[2,4,45,512]{3,0,2,1:T(2,128)(2,1)} copy(bf16[2,4,45,512]{3,2,0,1:T(8,128)(2,1)S(1)} %get-tuple-element.15) | data formatting | bytes 737280 | tf_op jit(solution)/shard_map/transpose | solution.py:619
  81.4 0.0 copy-done.1
  81.4 0.3 fusion
  81.7 2.4 %reshape.49 = f32[4,256,2,256]{3,2,1,0:T(2,128)} reshape(f32[4,256,512]{2,1,0:T(8,128)S(1)} %get-tuple-element.14) | data formatting | bytes 4194304 | tf_op jit(solution)/shard_map/convert_element_type | solution.py:704
  84.1 2.9 %copy.20 = f32[2,256,4,256]{3,2,1,0:T(4,128)S(1)} copy(f32[2,256,4,256]{3,0,1,2:T(2,128)} %bitcast.24) | data formatting | bytes 4194304 | tf_op jit(solution)/shard_map/convert_element_type | solution.py:704
  87.0 1.8 %copy.21 = f32[64,8,4,256]{3,1,2,0:T(8,128)} copy(f32[64,8,4,256]{3,2,1,0:T(4,128)S(1)} %bitcast.25) | data formatting | bytes 4194304
  88.8 1.7 %bitcast_convert_fusion = f32[1024,512]{1,0:T(8,128)} fusion(bf16[4,256,512]{2,1,0:T(8,128)(2,1)S(1)} %get-tuple-element.13), kind=kLoop, calls=%fused_computation | loop fusion | flops 524288 | bytes 3145728 | tf_op jit(solution)/shard_map/convert_element_type | solution.py:702
  90.5 0.6 copy.27
  (5 shorter events, 0.1 us)
Async XLA Ops:
  0.6 2.2 %copy-start.3 = (s32[2,5]{1,0:T(2,128)S(1)}, s32[2,5]{1,0:T(2,128)}, u32[]{:S(2)}) copy-start(s32[2,5]{1,0:T(2,128)} %param.8) | copy-start | bytes 124
  0.6 2.3 %copy-start.2 = (f32[2,5,8,13]{3,2,1,0:T(8,128)S(1)}, f32[2,5,8,13]{3,2,1,0:T(8,128)}, u32[]{:S(2)}) copy-start(f32[2,5,8,13]{3,2,1,0:T(8,128)} %param.9) | copy-start | bytes 12484
  0.7 2.5 %copy-start = (f32[8,512]{1,0:T(8,128)S(1)}, f32[8,512]{1,0:T(8,128)}, u32[]{:S(2)}) copy-start(f32[8,512]{1,0:T(8,128)} %basis.1) | copy-start | bytes 49156
  79.0 2.3 %copy-start.1 = (bf16[4,512,512]{2,1,0:T(8,128)(2,1)S(1)}, bf16[4,512,512]{2,1,0:T(8,128)(2,1)}, u32[]{:S(2)}) copy-start(bf16[4,512,512]{2,1,0:T(8,128)(2,1)} %get-tuple-element.11) | copy-start | bytes 6291460

commit v3 on v2

--- a/solution.py
+++ b/solution.py
@@ -151,6 +151,7 @@
 
 MESH = pl.DeviceIdType.MESH
 TILE = 16
+EDGE = 8
 CHUNK = 256
 GELU_SCALE = math.sqrt(2.0 / math.pi)
 GELU_CUBE = 0.044715
@@ -235,6 +236,7 @@
     fx,
     cx,
     mx,
+    packed,
     halo,
     buf,
     stage,
@@ -287,7 +289,6 @@
     lat_count, lon_count, rows, width, bands, count, basis_count, factor = sizes
     band_reach = (bands - 1) // 2
     total, padded_width, channels = fx.shape
-    pad = padded_width - width
     blocks = padded_width // TILE
     lat = lax.axis_index("lat")
     lon = lax.axis_index("lon")
@@ -344,26 +345,23 @@
     expand[...] = jnp.zeros_like(expand)
 
     def swap(own, which):
-        right = remote(
-            own.at[:, pl.ds(padded_width - TILE, TILE)],
-            halo.at[2 * which],
-            h_send.at[2 * which],
-            h_recv.at[2 * which],
-            nxt,
-        )
-        left = remote(
-            own.at[:, pl.ds(0, TILE)],
-            halo.at[2 * which + 1],
-            h_send.at[2 * which + 1],
-            h_recv.at[2 * which + 1],
-            prv,
-        )
-        return right, left
-
-    def fill(own, which):
-        stage[:, pad : pad + TILE] = halo[2 * which].astype(jnp.float32)
         stage[:, TILE : TILE + padded_width] = own[...].astype(jnp.float32)
-        stage[:, TILE + width : 2 * TILE + width] = halo[2 * which + 1].astype(jnp.float32)
+        ends = (stage[:, TILE + width - EDGE : TILE + width], stage[:, TILE : TILE + EDGE])
+        copies = []
+        for side, who in enumerate((nxt, prv)):
+            slot = 2 * which + side
+            packed[slot] = ends[side].reshape(total * EDGE, channels).astype(jnp.bfloat16)
+            copies.append(
+                remote(packed.at[slot], halo.at[slot], h_send.at[slot], h_recv.at[slot], who)
+            )
+        return copies
+
+    def fill(which):
+        edge = (total, EDGE, channels)
+        left = halo[2 * which].astype(jnp.float32).reshape(edge)
+        right = halo[2 * which + 1].astype(jnp.float32).reshape(edge)
+        stage[:, TILE - EDGE : TILE] = left
+        stage[:, TILE + width : TILE + width + EDGE] = right
         buf[band_reach : band_reach + total] = stage[...].astype(jnp.bfloat16)
 
     for copy in m_copies:
@@ -374,7 +372,7 @@
     swaps = swap(fx, 0)
     for copy in swaps:
         copy.wait()
-    fill(fx, 0)
+    fill(0)
 
     def view(i, b):
         window = buf[pl.ds(i, bands), TILE * b : TILE * (b + 3), :]
@@ -535,7 +533,7 @@
     advance(0)
     for copy in swaps:
         copy.wait()
-    fill(gx, 1)
+    fill(1)
 
     def back_row(i, carry):
         for b in range(blocks):
@@ -594,6 +592,14 @@
     gb[...] = jnp.sum(gb_z[...], axis=0)
     catch_up(7)
     wait(r_copies + g_copies)
+
+
+def widen_kernel(grads, giw, gow):
+    value = grads[0].astype(jnp.float32)
+    gow[...] = value[:CHUNK]
+    for cut in range(value.shape[1] // CHUNK):
+        lanes = slice(cut * CHUNK, (cut + 1) * CHUNK)
+        giw[lanes, :] = value[CHUNK:, lanes]
 
 
 def fused(fields_in, span, filters, basis, w_in, w_out, cotangent):
@@ -645,7 +651,8 @@
             pltpu.VMEM(cell_shape, bf16),
             pltpu.VMEM(cell_shape, bf16),
             pltpu.VMEM((total, basis_count, 128), f32),
-            pltpu.VMEM((4, total, TILE, channels), bf16),
+            pltpu.VMEM((4, total * EDGE, channels), bf16),
+            pltpu.VMEM((4, total * EDGE, channels), bf16),
             pltpu.VMEM((total + 2 * band_reach, window, channels), bf16),
             pltpu.VMEM((total, window, channels), f32),
             pltpu.VMEM((count, (total + 2 * band_reach) * basis_count, lanes), f32),
@@ -699,9 +706,19 @@
         ),
     )(split(fields_in), split(cotangent), coded, basis, w_in, w_out)
     result, grad_fields, grads, grad_basis = out
-    grad_out = grads[:, :CHUNK].reshape(hidden, channels).astype(f32)
-    grad_in = grads[:, CHUNK:].reshape(steps, CHUNK, channels // CHUNK, CHUNK)
-    grad_in = grad_in.transpose(2, 1, 0, 3).reshape(channels, hidden).astype(f32)
+    grad_in, grad_out = pl.pallas_call(
+        widen_kernel,
+        grid=(steps,),
+        out_shape=(
+            jax.ShapeDtypeStruct((channels, hidden), f32),
+            jax.ShapeDtypeStruct((hidden, channels), f32),
+        ),
+        in_specs=[pl.BlockSpec((1, piece, channels), lambda c: (c, 0, 0))],
+        out_specs=(
+            pl.BlockSpec((channels, CHUNK), lambda c: (0, c)),
+            pl.BlockSpec((CHUNK, channels), lambda c: (c, 0)),
+        ),
+    )(grads)
     return (joined(result), joined(grad_fields), grad_in, grad_out, grad_basis)
 
 
@@ -710,7 +727,7 @@
     share, left = divmod(fields_shape[1], lat_count * lon_count)
     pieces = CHUNK % (lat_count * max(1, lon_count // 2) * TILE) == 0
     even = lon_count % 2 == 0 and lon_count > 2 and fields_shape[0] % 4 == 0
-    wide = left == 0 and share >= TILE and (-share) % TILE <= TILE - 6
+    wide = left == 0 and share >= TILE and fields_shape[0] % 2 == 0
     return pieces and even and wide and lat_count > 1
 
 

time: 91.3 us -> 81.1 us (0.89)
  local copies, waits for them, and re-layouts: 12.4 us -> 4.28 us
  Pallas kernels: 75.9 us -> 74.1 us
    pallas_call x1, Pallas kernels: 75.9 us -> 70 us  [fused(): pl.pallas_call(functools.partial(block_kernel, sizes), out_shape=(jax.Sha...]
    convert_element_type x2 -> x0, local copies, waits for them, and re-layouts: 5.29 us -> none  [fused(): grad_in.transpose(2, 1, 0, 3).reshape(channels, hidden).astype(f32)]
    pallas_call x0 -> x1, Pallas kernels: none -> 4.14 us  [fused(): pl.pallas_call(widen_kernel, grid=(steps,), out_shape=(jax.ShapeDtypeStru...]
    unnamed x10 -> x5, local copies, waits for them, and re-layouts: 2.4 us -> 0.61 us
    convert_element_type x1 -> x0, other arithmetic: 1.68 us -> none  [fused(): grad_out = grads[:, :CHUNK].reshape(hidden, channels).astype(f32)]
    reshape x2, local copies, waits for them, and re-layouts: 2.08 us -> 1.08 us  [split(): cut = block.reshape(rows, lat_count, part, channels).swapaxes(0, 1)]
where the time goes in v3:
time: 81.1 us; the launch traced here: 80.7 us
  Pallas kernels  74.1 us (91%)
  local copies, waits for them, and re-layouts  4.28 us (5%)
  other arithmetic  1.59 us (2%)
    pallas_call x1, Pallas kernels, fused(): pl.pallas_call(functools.partial(block_kernel, sizes), out_shape=(jax.Sha...  70 us
    pallas_call x1, Pallas kernels, fused(): pl.pallas_call(widen_kernel, grid=(steps,), out_shape=(jax.ShapeDtypeStru...  4.14 us
    transpose x3, local copies, waits for them, and re-layouts, joined(): return block[:, :, :part].swapaxes(0, 1).reshape(rows, width, channels)  2.3 us

profile of v3, /device:TPU:0, one launch (start us, length us, event | category | flops | bytes accessed | tf_op | source)
XLA Modules:
  0.0 80.7 jit_solution(10067792473074606033)
XLA Ops:
  0.6 0.0 copy-start.1
  0.6 0.0 copy-start
  0.7 0.8 compare_convert_fusion
  1.5 0.8 multiply_bitcast_fusion
  2.2 0.1 copy.15
  2.4 0.1 copy.16
  2.5 1.0 %copy.22 = bf16[2,4,45,512]{3,2,0,1:T(8,128)(2,1)S(1)} copy(bf16[2,4,45,512]{3,0,2,1:T(2,128)(2,1)} %bitcast.19) | data formatting | bytes 737280 | tf_op jit(solution)/shard_map/reshape | solution.py:621
  3.6 0.0 copy-done.1
  3.7 0.0 copy-done
  3.7 70.0 %shard_map.110 = (bf16[4,2,48,512]{3,2,1,0:T(8,128)(2,1)S(1)}, bf16[4,2,48,512]{3,2,1,0:T(8,128)(2,1)S(1)}, bf16[4,512,512]{2,1,0:T(8,128)(2,1)}, f32[8,512]{1,0:T(8,128)S(1)}) custom-call(bf16[4,2,48,512]{3,2,1,0:T(8,128)(2,1)S(1)} %pad.11.f4, bf16[4,2,48,512]{3,2,1,0:T(8,128)(2,1)S(1)} %pad.12.c4, f32[2,8,128]{2,1,0:T(8,128)S(1)} %pad.13.mk, ...), custom_call_target="tpu_custom_call" | custom-call | tf_op jit(solution)/shard_map/pallas_call | solution.py:640
  73.7 0.1 slice_bitcast_fusion
  73.7 1.1 %copy.18 = bf16[2,4,45,512]{3,0,2,1:T(2,128)(2,1)} copy(bf16[2,4,45,512]{3,2,0,1:T(8,128)(2,1)S(1)} %get-tuple-element.17) | data formatting | bytes 737280 | tf_op jit(solution)/shard_map/transpose | solution.py:625
  74.9 1.1 %copy.17 = bf16[2,4,45,512]{3,0,2,1:T(2,128)(2,1)} copy(bf16[2,4,45,512]{3,2,0,1:T(8,128)(2,1)S(1)} %get-tuple-element.18) | data formatting | bytes 737280 | tf_op jit(solution)/shard_map/transpose | solution.py:625
  76.0 4.1 %shard_map.111 = (f32[512,1024]{1,0:T(8,128)}, f32[1024,512]{1,0:T(8,128)}) custom-call(bf16[4,512,512]{2,1,0:T(8,128)(2,1)} %get-tuple-element.13.grads), custom_call_target="tpu_custom_call" | custom-call | tf_op jit(solution)/shard_map/pallas_call | solution.py:709
  80.1 0.6 copy.24
  (5 shorter events, 0.1 us)
Async XLA Ops:
  0.6 2.9 %copy-start.1 = (bf16[2,180,512]{2,0,1:T(2,128)(2,1)S(1)}, bf16[2,180,512]{2,0,1:T(2,128)(2,1)}, u32[]{:S(2)}) copy-start(bf16[2,180,512]{2,0,1:T(2,128)(2,1)} %param.13) | copy-start | bytes 1105924
  0.6 3.0 %copy-start = (f32[8,512]{1,0:T(8,128)S(1)}, f32[8,512]{1,0:T(8,128)}, u32[]{:S(2)}) copy-start(f32[8,512]{1,0:T(8,128)} %basis.1) | copy-start | bytes 49156

commit v4 on v3

--- a/solution.py
+++ b/solution.py
@@ -326,12 +326,12 @@
         return copy
 
     mine = pl.ds(lat * rows, rows)
+    m_copies = [
+        remote(mk, mx.at[mine], m_send.at[n], m_recv.at[n], who) for n, who in enumerate(peers)
+    ]
     f_copies = [
         remote(f4.at[who[0]], fx.at[mine], f_send.at[n], f_recv.at[n], who)
         for n, who in enumerate(peers)
-    ]
-    m_copies = [
-        remote(mk, mx.at[mine], m_send.at[n], m_recv.at[n], who) for n, who in enumerate(peers)
     ]
     c_copies = [
         remote(c4.at[who[0]], cx.at[mine], c_send.at[n], c_recv.at[n], who)

time: 81.1 us -> 79.5 us (0.980)
  Pallas kernels: 74.1 us -> 72.6 us
    pallas_call x1, Pallas kernels: 70 us -> 68.4 us  [fused(): pl.pallas_call(functools.partial(block_kernel, sizes), out_shape=(jax.Sha...]
where the time goes in v4:
time: 79.5 us; the launch traced here: 79.2 us
  Pallas kernels  72.6 us (91%)
  local copies, waits for them, and re-layouts  4.28 us (5%)
  other arithmetic  1.59 us (2%)
    pallas_call x1, Pallas kernels, fused(): pl.pallas_call(functools.partial(block_kernel, sizes), out_shape=(jax.Sha...  68.4 us
    pallas_call x1, Pallas kernels, fused(): pl.pallas_call(widen_kernel, grid=(steps,), out_shape=(jax.ShapeDtypeStru...  4.14 us
    transpose x3, local copies, waits for them, and re-layouts, joined(): return block[:, :, :part].swapaxes(0, 1).reshape(rows, width, channels)  2.3 us

profile of v4, /device:TPU:0, one launch (start us, length us, event | category | flops | bytes accessed | tf_op | source)
XLA Modules:
  0.0 79.2 jit_solution(6478000544073646125)
XLA Ops:
  0.6 0.0 copy-start.1
  0.6 0.0 copy-start
  0.7 0.8 %compare_convert_fusion = f32[2,5,13]{2,1,0:T(8,128)S(1)} fusion(s32[2,5]{1,0:T(2,128)} %param.8, s32[13]{0:T(128)S(1)} %add_abs_fusion), kind=kLoop, calls=%fused_computation.5 | loop fusion | flops 260 | bytes 612 | tf_op jit(solution)/shard_map/convert_element_type | solution.py:34
  1.5 0.8 multiply_bitcast_fusion
  2.2 0.1 copy.15
  2.4 0.1 copy.16
  2.5 1.0 %copy.22 = bf16[2,4,45,512]{3,2,0,1:T(8,128)(2,1)S(1)} copy(bf16[2,4,45,512]{3,0,2,1:T(2,128)(2,1)} %bitcast.19) | data formatting | bytes 737280 | tf_op jit(solution)/shard_map/reshape | solution.py:621
  3.6 0.0 copy-done.1
  3.7 0.0 copy-done
  3.7 68.4 %shard_map.110 = (bf16[4,2,48,512]{3,2,1,0:T(8,128)(2,1)S(1)}, bf16[4,2,48,512]{3,2,1,0:T(8,128)(2,1)S(1)}, bf16[4,512,512]{2,1,0:T(8,128)(2,1)}, f32[8,512]{1,0:T(8,128)S(1)}) custom-call(bf16[4,2,48,512]{3,2,1,0:T(8,128)(2,1)S(1)} %pad.11.f4, bf16[4,2,48,512]{3,2,1,0:T(8,128)(2,1)S(1)} %pad.12.c4, f32[2,8,128]{2,1,0:T(8,128)S(1)} %pad.13.mk, ...), custom_call_target="tpu_custom_call" | custom-call | tf_op jit(solution)/shard_map/pallas_call | solution.py:640
  72.1 0.1 slice_bitcast_fusion
  72.2 1.1 %copy.18 = bf16[2,4,45,512]{3,0,2,1:T(2,128)(2,1)} copy(bf16[2,4,45,512]{3,2,0,1:T(8,128)(2,1)S(1)} %get-tuple-element.17) | data formatting | bytes 737280 | tf_op jit(solution)/shard_map/transpose | solution.py:625
  73.3 1.1 %copy.17 = bf16[2,4,45,512]{3,0,2,1:T(2,128)(2,1)} copy(bf16[2,4,45,512]{3,2,0,1:T(8,128)(2,1)S(1)} %get-tuple-element.18) | data formatting | bytes 737280 | tf_op jit(solution)/shard_map/transpose | solution.py:625
  74.4 4.1 %shard_map.111 = (f32[512,1024]{1,0:T(8,128)}, f32[1024,512]{1,0:T(8,128)}) custom-call(bf16[4,512,512]{2,1,0:T(8,128)(2,1)} %get-tuple-element.13.grads), custom_call_target="tpu_custom_call" | custom-call | tf_op jit(solution)/shard_map/pallas_call | solution.py:709
  78.6 0.6 copy.24
  (5 shorter events, 0.1 us)
Async XLA Ops:
  0.6 2.9 %copy-start.1 = (bf16[2,180,512]{2,0,1:T(2,128)(2,1)S(1)}, bf16[2,180,512]{2,0,1:T(2,128)(2,1)}, u32[]{:S(2)}) copy-start(bf16[2,180,512]{2,0,1:T(2,128)(2,1)} %param.13) | copy-start | bytes 1105924
  0.6 3.0 %copy-start = (f32[8,512]{1,0:T(8,128)S(1)}, f32[8,512]{1,0:T(8,128)}, u32[]{:S(2)}) copy-start(f32[8,512]{1,0:T(8,128)} %basis.1) | copy-start | bytes 49156
